TPU v7x, 32 devices: a whole 2x2x4 slice. The times are simulated.
32 devices in a mesh: orb: 8 (over y, x, core), grp: 4 (over z).
Axes of the slice: x: 2, y: 2, z: 4, core: 2. Of those that a mesh axis runs over, the one named last changes fastest.
Arguments:
- orbitals: bfloat16 [32, 64000], P(('orb', 'grp')), may hold values from -8 to 8
Outputs:
- projector: bfloat16 [32, 64000], P(('orb', 'grp'))
All inputs are finite; a program needn't handle non-finite values.
Results may differ from a plain program's by a relative error of at most 0.0012.
The roundings to bfloat16 on the way count: a program that leaves them out, or rounds other values in their place, can miss the bound.
Values may be sent and summed in bfloat16 or wider, within the bound.
A program may use at most 64 MiB of HBM per device.

v0:
```python
import functools
import math

import jax
import jax.numpy as jnp
import ml_dtypes
import numpy as np
from jax import lax
from jax.experimental import pallas as pl
from jax.experimental.pallas import tpu as pltpu
from jax.sharding import PartitionSpec as P

STEPS = 3
LANES = 128
AXES = ("orb", "grp")


def shifted(value, axis, steps):
    count = lax.axis_size(axis)
    pairs = [(source, (source + steps) % count) for source in range(count)]
    return lax.ppermute(value, axis, pairs)


def halves(table):
    high = table.astype(ml_dtypes.bfloat16)
    low = (table - high.astype(np.float64)).astype(ml_dtypes.bfloat16)
    return high, low


@functools.lru_cache(maxsize=None)
def tables(size):
    index = np.arange(size)
    angle = 2.0 * math.pi / size * (index[:, None] * index[None, :] % size)
    table = np.cos(angle) + np.sin(angle)
    plane = halves(np.kron(table, table))
    line = np.zeros((LANES, LANES))
    block = np.kron(np.eye(STEPS), table)
    line[: block.shape[0], : block.shape[0]] = block
    line = np.concatenate(halves(line), axis=1)
    signed = np.where(index <= size // 2, index, index - size)
    square = (2.0 * math.pi / size * signed) ** 2
    total = square[:, None, None] + square[None, :, None] + square[None, None, :]
    safe = np.where(total > 0, total, 1.0)
    kernel = np.where(total > 0, 4.0 * (1.0 - np.exp(-0.25 * total)) / safe, 1.0) / size**3
    kernel = np.tile(kernel.reshape(size * size, size), (1, STEPS))
    spread = np.zeros((size * size, LANES), np.float32)
    spread[:, : kernel.shape[1]] = kernel
    return plane[0], plane[1], line, spread


def split(value):
    high = value.astype(jnp.bfloat16)
    return high, (value - high.astype(jnp.float32)).astype(jnp.bfloat16)


def dot(left, right):
    return jnp.dot(left, right, preferred_element_type=jnp.float32)


def line_transform(value, line):
    high, low = split(value)
    both = dot(high, line)
    return both[:, :LANES] + (both[:, LANES:] + dot(low, line[:, :LANES]))


def plane_transform(store, high_ref, low_ref, pair, rows, block, scale=None):
    for start in range(0, rows, block):
        here = pl.ds(start, block)
        both = dot(high_ref[here, :], pair[...])
        out = both[:, :LANES] + (both[:, LANES:] + dot(low_ref[here, :], pair[:, :LANES]))
        store[here, :] = out if scale is None else out * scale[here, :]


def put_pair(pair, value):
    high, low = split(value)
    pair[:, :LANES] = high
    pair[:, LANES:] = low


def exchange_body(size, *refs):
    parts = refs[:STEPS]
    high_ref, low_ref, line_ref, kernel_ref, out_ref, store, pair = refs[STEPS:]
    rows = size * size
    block = rows // 5 if rows % 40 == 0 else rows
    values = [part[...].astype(jnp.float32) for part in parts]
    spare = jnp.zeros((rows, LANES - STEPS * size), jnp.float32)
    source = jnp.concatenate(values + [spare], axis=1)
    target = jnp.concatenate([values[0]] * STEPS + [spare], axis=1)
    line = line_ref[...]
    put_pair(pair, line_transform(target * source, line))
    plane_transform(store, high_ref, low_ref, pair, rows, block, kernel_ref)
    put_pair(pair, store[...])
    plane_transform(store, high_ref, low_ref, pair, rows, block)
    term = source * line_transform(store[...], line)
    total = -term[:, :size]
    for step in range(1, STEPS):
        total = total - term[:, step * size : (step + 1) * size]
    out_ref[...] = total.astype(jnp.bfloat16)


def exchange_of(parts, size):
    rows = size * size
    high, low, line, kernel = tables(size)
    vmem = pl.BlockSpec(memory_space=pltpu.VMEM)
    return pl.pallas_call(
        functools.partial(exchange_body, size),
        out_shape=jax.ShapeDtypeStruct((rows, size), jnp.bfloat16),
        in_specs=[vmem] * (STEPS + 4),
        out_specs=vmem,
        scratch_shapes=[
            pltpu.VMEM((rows, LANES), jnp.float32),
            pltpu.VMEM((rows, 2 * LANES), jnp.bfloat16),
        ],
        compiler_params=pltpu.CompilerParams(vmem_limit_bytes=48 * 2**20),
    )(*parts, high, low, line, kernel)


def factorize(margin):
    symmetric = 0.5 * (margin + margin.T)
    magnitude = jnp.abs(symmetric)
    gamma = jnp.mean(jnp.diagonal(magnitude)) + 1e-06
    regularized = jnp.diag(jnp.sum(magnitude, axis=1) + gamma) - symmetric
    factor = jnp.linalg.cholesky(regularized)
    identity = jnp.eye(symmetric.shape[0], dtype=jnp.float32)
    inverse = jax.scipy.linalg.solve_triangular(factor, identity, lower=True)
    return inverse.astype(jnp.bfloat16)


def to_slabs(flat, count, width):
    padded = jnp.pad(flat, ((0, 0), (0, count * width - flat.shape[1])))
    return lax.all_to_all(
        padded.reshape(count, width), AXES, split_axis=0, concat_axis=0, tiled=True
    )


def shards(orbitals):
    cells = orbitals.shape[1]
    size = round(cells ** (1.0 / 3.0))
    count = lax.axis_size("orb") * lax.axis_size("grp")
    width = -(-cells // (count * LANES)) * LANES
    parts = [orbitals] + [shifted(orbitals, "orb", step) for step in range(1, STEPS)]
    parts = [part.reshape(size * size, size) for part in parts]
    compact = exchange_of(parts, size).reshape(1, cells)
    orbital_slab = to_slabs(orbitals, count, width)
    exchange_slab = to_slabs(compact, count, width)
    margin = lax.dot_general(
        orbital_slab, exchange_slab, (((1,), (1,)), ((), ())), preferred_element_type=jnp.float32
    )
    inverse = factorize(lax.psum(margin, AXES) / cells)
    projected = dot(inverse, exchange_slab).astype(jnp.bfloat16)
    back = lax.all_to_all(projected, AXES, split_axis=0, concat_axis=0, tiled=True)
    return back.reshape(1, count * width)[:, :cells]


def solution(mesh):
    spec = P(AXES, None)
    return jax.shard_map(shards, mesh=mesh, in_specs=(spec,), out_specs=spec, check_vma=False)
```

profile of v0, /device:TPU:0, one launch (start us, length us, event | category | flops | bytes accessed | tf_op | source)
XLA Modules:
  0.0 116.1 jit_solution(13034973025863904480)
XLA Ops:
  0.0 1.2 %pad.7 = bf16[1,65536]{1,0:T(2,128)(2,1)S(1)} pad(bf16[1,64000]{1,0:T(2,128)(2,1)} %param.5, bf16[]{:T(256)} %constant.63.clone.1), padding=0_0x0_1536 | pad | bytes 259074 | tf_op jit(solution)/shard_map/jit(_pad)/pad | solution.py:130
  1.7 1.3 %reduce.9 = bf16[32,2048]{1,0:T(8,128)(2,1)S(1)} reduce(bf16[32,1,2048]{2,1,0:T(2,128)(2,1)S(1)} %bitcast.35, bf16[]{:T(256)} %broadcast.86), dimensions={1}, to_apply=%bitcast.reduce_sub_computation | reduce | bytes 262146 | tf_op jit(solution)/shard_map/all_to_all | solution.py:131
  3.0 0.7 reshape.53
  3.8 7.3 %all-to-all-start = ((bf16[32,2,1024]{2,1,0:T(2,128)(2,1)}), bf16[32,2,1024]{2,1,0:T(2,128)(2,1)S(1)}, u32[]{:S(2)}, u32[]{:S(2)}) async-start(bf16[32,2,1024]{2,1,0:T(2,128)(2,1)} %reshape.53), calls=%async_computation | async-start | bytes 262144 | tf_op jit(solution)/shard_map/all_to_all | solution.py:131
  11.4 1.7 %collective-permute-start.1 = (bf16[1,64000]{1,0:T(2,128)(2,1)}, bf16[1,64000]{1,0:T(2,128)(2,1)S(1)}, u32[]{:S(2)}, u32[]{:S(2)}) collective-permute-start(bf16[1,64000]{1,0:T(2,128)(2,1)} %param.5), channel_id=1, source_target_pairs={{0,8},{4,12},{8,16},{12,20},{16,24},{20,28},{24,0},{28,4},{1,9},{5... | collective-permute-start | bytes 384008 | tf_op jit(solution)/shard_map/ppermute | solution.py:21
  13.0 1.7 %reduce.6 = bf16[64000]{0:T(1024)(128)(2,1)S(1)} reduce(bf16[1,64000]{1,0:T(2,128)(2,1)} %param.5, bf16[]{:T(256)} %constant.93), dimensions={0}, to_apply=%param.5.reduce_sub_computation | reduce | bytes 256002 | tf_op args[0]
  15.3 6.1 %collective-permute-done = bf16[1,64000]{1,0:T(2,128)(2,1)S(1)} collective-permute-done((bf16[1,64000]{1,0:T(2,128)(2,1)}, bf16[1,64000]{1,0:T(2,128)(2,1)S(1)}, u32[]{:S(2)}, u32[]{:S(2)}) %collective-permute-start) | collective-permute-done | bytes 128032 | tf_op jit(solution)/shard_map/ppermute | solution.py:21
  21.4 0.7 reduce.7
  22.8 0.7 reduce.8
  24.2 1.1 copy-done
  25.3 0.8 copy-done.1
  26.2 11.4 %shard_map.55 = bf16[1600,40]{1,0:T(8,128)(2,1)S(1)} custom-call(bf16[1600,40]{1,0:T(8,128)(2,1)S(1)} %reshape.39.refs_0_, bf16[1600,40]{1,0:T(8,128)(2,1)S(1)} %reshape.40.refs_1_, bf16[1600,40]{1,0:T(8,128)(2,1)S(1)} %reshape.41.refs_2_, bf16[1600,1600]{1,0:T(8,128)(2,1)} %constant.71.clone.refs_3_, bf16[1600,1600]{1,0:T(8,128)(2,1)} %constant.72.clone.refs_4_, ...), custom_call_target="tpu_custom_call" | custom-call | tf_op jit(solution)/shard_map/pallas_call | solution.py:105
  38.4 1.3 %reduce.10 = bf16[32,2048]{1,0:T(8,128)(2,1)S(1)} reduce(bf16[32,1,2048]{2,1,0:T(2,128)(2,1)S(1)} %bitcast.34, bf16[]{:T(256)} %broadcast.86), dimensions={1}, to_apply=%bitcast.1.reduce_sub_computation | reduce | bytes 262146 | tf_op jit(solution)/shard_map/all_to_all | solution.py:131
  39.7 0.7 reshape.55
  40.4 5.4 %all-to-all-start.1 = ((bf16[32,2,1024]{2,1,0:T(2,128)(2,1)}), bf16[32,2,1024]{2,1,0:T(2,128)(2,1)S(1)}, u32[]{:S(2)}, u32[]{:S(2)}) async-start(bf16[32,2,1024]{2,1,0:T(2,128)(2,1)} %reshape.55), calls=%async_computation.1 | async-start | bytes 262144 | tf_op jit(solution)/shard_map/all_to_all | solution.py:131
  46.0 8.1 %all-to-all-done.1 = bf16[32,2,1024]{2,1,0:T(2,128)(2,1)S(1)} async-done(((bf16[32,2,1024]{2,1,0:T(2,128)(2,1)}), bf16[32,2,1024]{2,1,0:T(2,128)(2,1)S(1)}, u32[]{:S(2)}, u32[]{:S(2)}) %all-to-all-start.1) | async-done | bytes 131104 | tf_op jit(solution)/shard_map/all_to_all | solution.py:131
  54.4 37.3 %psum.7 = f32[32,32]{0,1:T(8,128)S(1)} all-reduce(f32[32,32]{0,1:T(8,128)S(1)} %fusion.2), channel_id=1, replica_groups=mesh['orb'=8,'grp'=4] {'orb','grp'}, use_global_device_ids=true, to_apply=%region_0.1 | all-reduce | flops 1024 | bytes 8192 | tf_op jit(solution)/shard_map/psum | solution.py:149
  91.9 0.7 gather_fusion
  94.1 2.9 %cholesky.17 = f32[32,32]{1,0:T(8,128)S(1)} custom-call(f32[32,32]{1,0:T(8,128)S(1)} %fusion.10), custom_call_target="Cholesky" | custom-call | tf_op jit(solution)/shard_map/jit(cholesky)/cholesky | solution.py:123
  97.0 0.6 compare_reduce_fusion
  97.7 0.7 fusion.8
  98.3 2.4 %custom-call.7 = f32[1,32,32]{1,2,0:T(8,128)S(1)} custom-call(f32[1,32,32]{2,1,0:T(8,128)S(1)} %fusion.8), custom_call_target="InvertDiagBlocksLowerTriangular" | custom-call | tf_op jit(solution)/shard_map/jit(_solve_triangular)/triangular_solve | solution.py:125
  101.9 13.1 %all_to_all.33 = bf16[32,2,1024]{2,1,0:T(2,128)(2,1)S(1)} all-to-all(bf16[32,2,1024]{2,1,0:T(2,128)(2,1)S(1)} %reshape.57), channel_id=1, replica_groups=mesh['orb'=8,'grp'=4] {'orb','grp'}, dimensions={0} | all-to-all | bytes 262144 | tf_op jit(solution)/shard_map/all_to_all | solution.py:151
  115.1 1.0 slice.18
  (29 shorter events, 6.1 us)
Async XLA Ops:
  3.8 36.7 %all-to-all-start = ((bf16[32,2,1024]{2,1,0:T(2,128)(2,1)}), bf16[32,2,1024]{2,1,0:T(2,128)(2,1)S(1)}, u32[]{:S(2)}, u32[]{:S(2)}) async-start(bf16[32,2,1024]{2,1,0:T(2,128)(2,1)} %reshape.53), calls=%async_computation | async-start | bytes 262144 | tf_op jit(solution)/shard_map/all_to_all | solution.py:131
  11.1 10.4 %collective-permute-start = (bf16[1,64000]{1,0:T(2,128)(2,1)}, bf16[1,64000]{1,0:T(2,128)(2,1)S(1)}, u32[]{:S(2)}, u32[]{:S(2)}) collective-permute-start(bf16[1,64000]{1,0:T(2,128)(2,1)} %param.5), channel_id=1, source_target_pairs={{0,4},{4,8},{8,12},{12,16},{16,20},{20,24},{24,28},{28,0},{1,5},{5... | collective-permute-start | bytes 384008 | tf_op jit(solution)/shard_map/ppermute | solution.py:21
  11.4 11.4 %collective-permute-start.1 = (bf16[1,64000]{1,0:T(2,128)(2,1)}, bf16[1,64000]{1,0:T(2,128)(2,1)S(1)}, u32[]{:S(2)}, u32[]{:S(2)}) collective-permute-start(bf16[1,64000]{1,0:T(2,128)(2,1)} %param.5), channel_id=1, source_target_pairs={{0,8},{4,12},{8,16},{12,20},{16,24},{20,28},{24,0},{28,4},{1,9},{5... | collective-permute-start | bytes 384008 | tf_op jit(solution)/shard_map/ppermute | solution.py:21
  24.2 1.1 copy-start
  25.3 0.8 copy-start.1
  40.4 13.7 %all-to-all-start.1 = ((bf16[32,2,1024]{2,1,0:T(2,128)(2,1)}), bf16[32,2,1024]{2,1,0:T(2,128)(2,1)S(1)}, u32[]{:S(2)}, u32[]{:S(2)}) async-start(bf16[32,2,1024]{2,1,0:T(2,128)(2,1)} %reshape.55), calls=%async_computation.1 | async-start | bytes 262144 | tf_op jit(solution)/shard_map/all_to_all | solution.py:131
where the time goes:
time: 117 us; the launch traced here: 116 us
  blocking collectives  50.4 us (43%)
  starting transfers between devices  14.7 us (13%)
  waiting for transfers between devices  14.2 us (12%)
  other arithmetic  13.8 us (12%)
  Pallas kernels  11.4 us (10%)
  local copies, waits for them, and re-layouts  10 us (9%)
    psum x1, blocking collectives, shards(): inverse = factorize(lax.psum(margin, AXES) / cells)  37.3 us
    all_to_all x1, blocking collectives, shards(): lax.all_to_all(projected, AXES, split_axis=0, concat_axis=0, tiled=True)  13.1 us
    all_to_all x2, starting transfers between devices, to_slabs(): lax.all_to_all(padded.reshape(count, width), AXES, split_axis=0, concat_a...  12.7 us
    pallas_call x1, Pallas kernels, exchange_of(): pl.pallas_call(functools.partial(exchange_body, size), out_shape=jax.Shap...  11.4 us
    all_to_all x2, waiting for transfers between devices, to_slabs(): lax.all_to_all(padded.reshape(count, width), AXES, split_axis=0, concat_a...  8.11 us
    ppermute x2, waiting for transfers between devices, shifted(): return lax.ppermute(value, axis, pairs)  6.12 us
    unnamed x10, local copies, waits for them, and re-layouts  3.81 us
    another operation x3, other arithmetic, factorize(): factor = jnp.linalg.cholesky(regularized)  3.6 us
  transfers between devices with their start and end apart: 4, of which 2 were waited for; matrix products, arithmetic and copies ran while one was open for 7% of the time, Pallas kernels for 10%

commit v1 on v0

--- a/solution.py
+++ b/solution.py
@@ -133,16 +133,167 @@
     )
 
 
+def invert(mat, work, n, cells):
+    lanes = mat.shape[2]
+    row = lax.broadcasted_iota(jnp.int32, (n, lanes), 0)
+    column = lax.broadcasted_iota(jnp.int32, (n, lanes), 1)
+    diagonal = row == column
+    symmetric = mat[:, 0, :] * (0.5 / cells)
+    magnitude = jnp.abs(symmetric)
+    gamma = jnp.sum(jnp.where(diagonal, magnitude, 0.0)) / n + 1e-06
+    total = jnp.sum(magnitude, axis=1, keepdims=True) + gamma
+    work[:, :lanes] = jnp.where(diagonal, total, 0.0) - symmetric
+    work[:, lanes:] = jnp.where(diagonal, 1.0, 0.0)
+    wide_row = lax.broadcasted_iota(jnp.int32, (n, 1), 0)
+
+    def eliminate(step, carry):
+        pivot_row = work[pl.ds(step, 1), :]
+        value = work[...]
+        left = jnp.where(column == step, value[:, :lanes], 0.0)
+        entries = jnp.sum(left, axis=1, keepdims=True)
+        pivot = jnp.sum(
+            jnp.where(column[:1] == step, pivot_row[:, :lanes], 0.0), axis=1, keepdims=True
+        )
+        ratio = jnp.where(wide_row > step, entries / pivot, 0.0)
+        work[...] = value - ratio * pivot_row
+        return carry
+
+    lax.fori_loop(0, n, eliminate, 0)
+    pivots = jnp.sum(jnp.where(diagonal, work[:, :lanes], 0.0), axis=1, keepdims=True)
+    return (work[:, lanes:] * lax.rsqrt(pivots)).astype(jnp.bfloat16)
+
+
+def flatten(wide, ref):
+    wide[...] = ref[...].astype(jnp.float32)
+    pieces = [wide[:, line, :] for line in range(wide.shape[1])]
+    return jnp.concatenate(pieces, axis=1).astype(jnp.bfloat16)
+
+
+def tail_body(count, groups, cells, orbital, exchange, back, orb_slab, exc_slab, wide, part, got,
+              line, mat, work, proj, send_sem, recv_sem):
+    n = count
+    lanes = mat.shape[2]
+    me = lax.axis_index("orb") * groups + lax.axis_index("grp")
+
+    def device(step):
+        other = lax.rem(me + step, count)
+        return other, (lax.div(other, groups), lax.rem(other, groups))
+
+    def each(action):
+        def body(step, carry):
+            action(*device(step))
+            return carry
+
+        lax.fori_loop(1, count, body, 0)
+
+    def send(source, target, slot, other, place):
+        pltpu.make_async_remote_copy(
+            src_ref=source,
+            dst_ref=target.at[me],
+            send_sem=send_sem.at[slot],
+            recv_sem=recv_sem.at[slot],
+            device_id=place,
+            device_id_type=pl.DeviceIdType.MESH,
+        ).start()
+
+    def wait(target, slot):
+        most = target.at[pl.ds(0, count - 1)]
+        pltpu.make_async_copy(most, most, recv_sem.at[slot]).wait()
+        pltpu.make_async_copy(most, most, send_sem.at[slot]).wait()
+
+    barrier = pltpu.get_barrier_semaphore()
+    each(
+        lambda other, place: pl.semaphore_signal(
+            barrier, inc=1, device_id=place, device_id_type=pl.DeviceIdType.MESH
+        )
+    )
+    pl.semaphore_wait(barrier, count - 1)
+
+    def slabs(other, place):
+        send(exchange.at[other], exc_slab, 0, other, place)
+        send(orbital.at[other], orb_slab, 1, other, place)
+
+    each(slabs)
+    exc_slab[pl.ds(me, 1)] = exchange[pl.ds(me, 1)]
+    orb_slab[pl.ds(me, 1)] = orbital[pl.ds(me, 1)]
+    wait(exc_slab, 0)
+    wait(orb_slab, 1)
+    exc = flatten(wide, exc_slab)
+    orb = flatten(wide, orb_slab)
+    turned = (((1,), (1,)), ((), ()))
+    both = lax.dot_general(orb, exc, turned, preferred_element_type=jnp.float32)
+    both = both + lax.dot_general(exc, orb, turned, preferred_element_type=jnp.float32)
+    if lanes > n:
+        both = jnp.concatenate([both, jnp.zeros((n, lanes - n), jnp.float32)], axis=1)
+    part[...] = jnp.broadcast_to(both[:, None, :], part.shape)
+    each(lambda other, place: send(part.at[other], got, 2, other, place))
+    got[pl.ds(me, 1)] = part[pl.ds(me, 1)]
+    wait(got, 2)
+    line[...] = jnp.sum(got[...], axis=0)
+    each(lambda other, place: send(line, mat, 3, other, place))
+    mat[pl.ds(me, 1)] = line[...][None]
+    wait(mat, 3)
+    inverse = invert(mat, work, n, cells)[:, :n]
+    projected = dot(inverse, exc)
+    for index in range(wide.shape[1]):
+        wide[:, index, :] = projected[:, index * LANES : (index + 1) * LANES]
+    proj[...] = wide[...].astype(jnp.bfloat16)
+    each(lambda other, place: send(proj.at[other], back, 4, other, place))
+    back[pl.ds(me, 1)] = proj[pl.ds(me, 1)]
+    wait(back, 4)
+
+
+def tail(orbital, exchange, cells):
+    count, lines, _ = orbital.shape
+    groups = lax.axis_size("grp")
+    lanes = -(-count // LANES) * LANES
+    vmem = pl.BlockSpec(memory_space=pltpu.VMEM)
+    slab = pltpu.VMEM(orbital.shape, jnp.bfloat16)
+    rows = pltpu.VMEM((count, 8, lanes), jnp.float32)
+    return pl.pallas_call(
+        functools.partial(tail_body, count, groups, cells),
+        out_shape=jax.ShapeDtypeStruct(orbital.shape, jnp.bfloat16),
+        in_specs=[vmem] * 2,
+        out_specs=vmem,
+        scratch_shapes=[
+            slab,
+            slab,
+            pltpu.VMEM(orbital.shape, jnp.float32),
+            rows,
+            rows,
+            pltpu.VMEM((8, lanes), jnp.float32),
+            rows,
+            pltpu.VMEM((count, 2 * lanes), jnp.float32),
+            slab,
+            pltpu.SemaphoreType.DMA((5,)),
+            pltpu.SemaphoreType.DMA((5,)),
+        ],
+        compiler_params=pltpu.CompilerParams(
+            collective_id=0, has_side_effects=True, vmem_limit_bytes=56 * 2**20
+        ),
+    )(orbital, exchange)
+
+
+def to_pieces(flat, count, lines):
+    tall = flat.reshape(-1, LANES)
+    padded = jnp.pad(tall, ((0, count * lines - tall.shape[0]), (0, 0)))
+    return padded.reshape(count, lines, LANES)
+
+
 def shards(orbitals):
     cells = orbitals.shape[1]
     size = round(cells ** (1.0 / 3.0))
     count = lax.axis_size("orb") * lax.axis_size("grp")
-    width = -(-cells // (count * LANES)) * LANES
     parts = [orbitals] + [shifted(orbitals, "orb", step) for step in range(1, STEPS)]
     parts = [part.reshape(size * size, size) for part in parts]
-    compact = exchange_of(parts, size).reshape(1, cells)
+    compact = exchange_of(parts, size)
+    if count <= LANES:
+        lines = -(-cells // (count * LANES * 16)) * 16
+        back = tail(to_pieces(orbitals, count, lines), to_pieces(compact, count, lines), cells)
+        return back.reshape(count * lines, LANES)[: cells // LANES].reshape(1, cells)
+    width = -(-cells // (count * LANES)) * LANES
     orbital_slab = to_slabs(orbitals, count, width)
-    exchange_slab = to_slabs(compact, count, width)
+    exchange_slab = to_slabs(compact.reshape(1, cells), count, width)
     margin = lax.dot_general(
         orbital_slab, exchange_slab, (((1,), (1,)), ((), ())), preferred_element_type=jnp.float32
     )

time: 117 us -> 66.1 us (0.56)
  blocking collectives: 50.4 us -> 0 us
  Pallas kernels: 11.4 us -> 48.2 us
  starting transfers between devices: 14.7 us -> 2.97 us
  other arithmetic: 13.8 us -> 3.17 us
  waiting for transfers between devices: 14.2 us -> 3.8 us
  local copies, waits for them, and re-layouts: 10 us -> 7.56 us
    psum x1 -> x0, blocking collectives: 37.3 us -> none  [shards(): inverse = factorize(lax.psum(margin, AXES) / cells)]
    pallas_call x0 -> x1, Pallas kernels: none -> 36.9 us  [tail(): pl.pallas_call(functools.partial(tail_body, count, groups, cells), out_sh...]
    all_to_all x1 -> x0, blocking collectives: 13.1 us -> none  [shards(): lax.all_to_all(projected, AXES, split_axis=0, concat_axis=0, tiled=True)]
    all_to_all x2 -> x0, starting transfers between devices: 12.7 us -> none  [to_slabs(): lax.all_to_all(padded.reshape(count, width), AXES, split_axis=0, concat_a...]
    all_to_all x2 -> x0, waiting for transfers between devices: 8.11 us -> none  [to_slabs(): lax.all_to_all(padded.reshape(count, width), AXES, split_axis=0, concat_a...]
    another operation x5 -> x0, other arithmetic: 6.68 us -> none  [the longest x3 3.6 us: factorize(): factor = jnp.linalg.cholesky(regularized)]
    all_to_all x3 -> x0, other arithmetic: 3.17 us -> none  [the longest x2 2.58 us: to_slabs(): lax.all_to_all(padded.reshape(count, width), AXES, split_axis=0, concat_a...]
    ppermute x2, waiting for transfers between devices: 6.12 us -> 3.8 us  [shifted(): return lax.ppermute(value, axis, pairs)]
  transfers between devices with their start and end apart: 4 -> 2, of which waited for: 2 -> 2; matrix products, arithmetic and copies ran while one was open for 7% -> 7% of each run, Pallas kernels for 10% -> 0%
where the time goes in v1:
time: 66.1 us; the launch traced here: 65.8 us
  Pallas kernels  48.2 us (73%)
  local copies, waits for them, and re-layouts  7.56 us (11%)
  waiting for transfers between devices  3.8 us (6%)
  other arithmetic  3.17 us (5%)
  starting transfers between devices  2.97 us (4%)
    pallas_call x1, Pallas kernels, tail(): pl.pallas_call(functools.partial(tail_body, count, groups, cells), out_sh...  36.9 us
    pallas_call x1, Pallas kernels, exchange_of(): pl.pallas_call(functools.partial(exchange_body, size), out_shape=jax.Shap...  11.4 us
    ppermute x2, waiting for transfers between devices, shifted(): return lax.ppermute(value, axis, pairs)  3.8 us
    unnamed x6, local copies, waits for them, and re-layouts  3.79 us
    ppermute x2, starting transfers between devices, shifted(): return lax.ppermute(value, axis, pairs)  2.97 us
    reshape x3, local copies, waits for them, and re-layouts, shards(): parts = [part.reshape(size * size, size) for part in parts]  1.84 us
    unnamed x1, other arithmetic  1.67 us
    ppermute x2, other arithmetic, shifted(): return lax.ppermute(value, axis, pairs)  1.5 us
  transfers between devices with their start and end apart: 2, of which 2 were waited for; matrix products, arithmetic and copies ran while one was open for 7% of the time, Pallas kernels for 0%

profile of v1, /device:TPU:0, one launch (start us, length us, event | category | flops | bytes accessed | tf_op | source)
XLA Modules:
  0.0 65.8 jit_solution(4423769851884374987)
XLA Ops:
  0.0 0.5 collective-permute-start
  0.5 2.5 %collective-permute-start.1 = (bf16[1,64000]{1,0:T(2,128)(2,1)}, bf16[1,64000]{1,0:T(2,128)(2,1)S(1)}, u32[]{:S(2)}, u32[]{:S(2)}) collective-permute-start(bf16[1,64000]{1,0:T(2,128)(2,1)} %param.5), channel_id=1, source_target_pairs={{0,8},{4,12},{8,16},{12,20},{16,24},{20,28},{24,0},{28,4},{1,9},{5... | collective-permute-start | bytes 384008 | tf_op jit(solution)/shard_map/ppermute | solution.py:21
  3.0 1.7 %reduce = bf16[64000]{0:T(1024)(128)(2,1)S(1)} reduce(bf16[1,64000]{1,0:T(2,128)(2,1)} %param.5, bf16[]{:T(256)} %constant.20), dimensions={0}, to_apply=%param.5.reduce_sub_computation | reduce | bytes 256002 | tf_op args[0]
  4.6 0.6 reshape.29.refs_0_
  5.3 0.7 %pad.7 = bf16[512,128]{1,0:T(8,128)(2,1)} pad(bf16[500,128]{1,0:T(8,128)(2,1)S(1)} %bitcast.10, bf16[]{:T(256)} %constant.10.clone.1), padding=0_12x0_0 | pad | bytes 259074 | tf_op jit(solution)/shard_map/jit(_pad)/pad | solution.py:279
  5.9 3.5 %collective-permute-done = bf16[1,64000]{1,0:T(2,128)(2,1)S(1)} collective-permute-done((bf16[1,64000]{1,0:T(2,128)(2,1)}, bf16[1,64000]{1,0:T(2,128)(2,1)S(1)}, u32[]{:S(2)}, u32[]{:S(2)}) %collective-permute-start) | collective-permute-done | bytes 128032 | tf_op jit(solution)/shard_map/ppermute | solution.py:21
  9.4 0.7 %reduce.2 = bf16[64000]{0:T(1024)(128)(2,1)S(1)} reduce(bf16[1,64000]{1,0:T(2,128)(2,1)S(1)} %collective-permute-done, bf16[]{:T(256)} %constant.20), dimensions={0}, to_apply=%ppermute.6.reduce_sub_computation | reduce | bytes 256002 | tf_op jit(solution)/shard_map/ppermute | solution.py:21
  10.2 0.6 reshape.30.refs_1_
  10.8 0.3 collective-permute-done.1
  11.1 0.7 %reduce.3 = bf16[64000]{0:T(1024)(128)(2,1)S(1)} reduce(bf16[1,64000]{1,0:T(2,128)(2,1)S(1)} %collective-permute-done.1, bf16[]{:T(256)} %constant.20), dimensions={0}, to_apply=%ppermute.7.reduce_sub_computation | reduce | bytes 256002 | tf_op jit(solution)/shard_map/ppermute | solution.py:21
  11.9 0.6 reshape.31.refs_2_
  12.5 0.0 copy-start
  12.5 1.1 %copy-done = f32[1600,128]{1,0:T(8,128)S(1)} copy-done((f32[1600,128]{1,0:T(8,128)S(1)}, f32[1600,128]{1,0:T(8,128)}, u32[]{:S(2)}) %copy-start) | copy-done | bytes 819224
  13.6 0.0 copy-start.1
  13.6 0.8 %copy-done.1 = bf16[128,256]{1,0:T(8,128)(2,1)S(1)} copy-done((bf16[128,256]{1,0:T(8,128)(2,1)S(1)}, bf16[128,256]{1,0:T(8,128)(2,1)}, u32[]{:S(2)}) %copy-start.1) | copy-done | bytes 65560
  14.5 11.4 %shard_map.55 = bf16[1600,40]{1,0:T(8,128)(2,1)S(1)} custom-call(bf16[1600,40]{1,0:T(8,128)(2,1)S(1)} %reshape.29.refs_0_, bf16[1600,40]{1,0:T(8,128)(2,1)S(1)} %reshape.30.refs_1_, bf16[1600,40]{1,0:T(8,128)(2,1)S(1)} %reshape.31.refs_2_, bf16[1600,1600]{1,0:T(8,128)(2,1)} %constant.11.clone.refs_3_, bf16[1600,1600]{1,0:T(8,128)(2,1)} %constant.12.clone.refs_4_, ...), custom_call_target="tpu_custom_call" | custom-call | tf_op jit(solution)/shard_map/pallas_call | solution.py:105
  25.8 0.6 reshape.32
  26.5 0.7 pad.8
  27.1 36.9 %shard_map.56 = bf16[32,16,128]{2,1,0:T(8,128)(2,1)} custom-call(bf16[32,16,128]{2,1,0:T(8,128)(2,1)} %bitcast.11, bf16[32,16,128]{2,1,0:T(8,128)(2,1)} %bitcast.12), custom_call_target="tpu_custom_call" | custom-call | tf_op jit(solution)/shard_map/pallas_call | solution.py:253
  64.0 0.9 %slice_bitcast_fusion = bf16[1,1,500,128]{3,2,1,0:T(8,128)(2,1)S(1)} fusion(bf16[512,128]{1,0:T(8,128)(2,1)} %bitcast.13), kind=kLoop, calls=%fused_computation.1 | loop fusion | bytes 256000
  64.9 0.9 %copy.8 = bf16[1,1,500,128]{3,1,2,0:T(2,128)(2,1)} copy(bf16[1,1,500,128]{3,2,1,0:T(8,128)(2,1)S(1)} %slice_bitcast_fusion) | data formatting | bytes 256000
Async XLA Ops:
  0.0 9.4 %collective-permute-start = (bf16[1,64000]{1,0:T(2,128)(2,1)}, bf16[1,64000]{1,0:T(2,128)(2,1)S(1)}, u32[]{:S(2)}, u32[]{:S(2)}) collective-permute-start(bf16[1,64000]{1,0:T(2,128)(2,1)} %param.5), channel_id=1, source_target_pairs={{0,4},{4,8},{8,12},{12,16},{16,20},{20,24},{24,28},{28,0},{1,5},{5... | collective-permute-start | bytes 384008 | tf_op jit(solution)/shard_map/ppermute | solution.py:21
  0.5 10.7 %collective-permute-start.1 = (bf16[1,64000]{1,0:T(2,128)(2,1)}, bf16[1,64000]{1,0:T(2,128)(2,1)S(1)}, u32[]{:S(2)}, u32[]{:S(2)}) collective-permute-start(bf16[1,64000]{1,0:T(2,128)(2,1)} %param.5), channel_id=1, source_target_pairs={{0,8},{4,12},{8,16},{12,20},{16,24},{20,28},{24,0},{28,4},{1,9},{5... | collective-permute-start | bytes 384008 | tf_op jit(solution)/shard_map/ppermute | solution.py:21
  12.5 1.1 %copy-start = (f32[1600,128]{1,0:T(8,128)S(1)}, f32[1600,128]{1,0:T(8,128)}, u32[]{:S(2)}) copy-start(f32[1600,128]{1,0:T(8,128)} %constant.14.clone.refs_6_) | copy-start | bytes 2457604
  13.6 0.8 %copy-start.1 = (bf16[128,256]{1,0:T(8,128)(2,1)S(1)}, bf16[128,256]{1,0:T(8,128)(2,1)}, u32[]{:S(2)}) copy-start(bf16[128,256]{1,0:T(8,128)(2,1)} %constant.13.clone.refs_5_) | copy-start | bytes 196612

commit v2 on v1

--- a/solution.py
+++ b/solution.py
@@ -133,34 +133,23 @@
     )
 
 
-def invert(mat, work, n, cells):
-    lanes = mat.shape[2]
-    row = lax.broadcasted_iota(jnp.int32, (n, lanes), 0)
-    column = lax.broadcasted_iota(jnp.int32, (n, lanes), 1)
+def invert(symmetric, n):
+    row = lax.broadcasted_iota(jnp.int32, (n, n), 0)
+    column = lax.broadcasted_iota(jnp.int32, (n, n), 1)
     diagonal = row == column
-    symmetric = mat[:, 0, :] * (0.5 / cells)
     magnitude = jnp.abs(symmetric)
     gamma = jnp.sum(jnp.where(diagonal, magnitude, 0.0)) / n + 1e-06
     total = jnp.sum(magnitude, axis=1, keepdims=True) + gamma
-    work[:, :lanes] = jnp.where(diagonal, total, 0.0) - symmetric
-    work[:, lanes:] = jnp.where(diagonal, 1.0, 0.0)
-    wide_row = lax.broadcasted_iota(jnp.int32, (n, 1), 0)
-
-    def eliminate(step, carry):
-        pivot_row = work[pl.ds(step, 1), :]
-        value = work[...]
-        left = jnp.where(column == step, value[:, :lanes], 0.0)
-        entries = jnp.sum(left, axis=1, keepdims=True)
-        pivot = jnp.sum(
-            jnp.where(column[:1] == step, pivot_row[:, :lanes], 0.0), axis=1, keepdims=True
-        )
-        ratio = jnp.where(wide_row > step, entries / pivot, 0.0)
-        work[...] = value - ratio * pivot_row
-        return carry
-
-    lax.fori_loop(0, n, eliminate, 0)
-    pivots = jnp.sum(jnp.where(diagonal, work[:, :lanes], 0.0), axis=1, keepdims=True)
-    return (work[:, lanes:] * lax.rsqrt(pivots)).astype(jnp.bfloat16)
+    regularized = jnp.where(diagonal, total, 0.0) - symmetric
+    value = jnp.concatenate([regularized, jnp.where(diagonal, 1.0, 0.0)], axis=1)
+    below = lax.broadcasted_iota(jnp.int32, (n, 1), 0)
+    for step in range(n - 1):
+        here = slice(step, step + 1)
+        scaled = value[here, :] / value[here, here]
+        ratio = jnp.where(below > step, value[:, here], 0.0)
+        value = value - ratio * scaled
+    pivots = jnp.sum(jnp.where(diagonal, value[:, :n], 0.0), axis=1, keepdims=True)
+    return (value[:, n:] * lax.rsqrt(pivots)).astype(jnp.bfloat16)
 
 
 def flatten(wide, ref):
@@ -170,13 +159,13 @@
 
 
 def tail_body(count, groups, cells, orbital, exchange, back, orb_slab, exc_slab, wide, part, got,
-              line, mat, work, proj, send_sem, recv_sem):
+              proj, send_sem, recv_sem):
     n = count
-    lanes = mat.shape[2]
     me = lax.axis_index("orb") * groups + lax.axis_index("grp")
 
     def device(step):
-        other = lax.rem(me + step, count)
+        other = me + step
+        other = jnp.where(other >= count, other - count, other)
         return other, (lax.div(other, groups), lax.rem(other, groups))
 
     def each(action):
@@ -223,33 +212,29 @@
     turned = (((1,), (1,)), ((), ()))
     both = lax.dot_general(orb, exc, turned, preferred_element_type=jnp.float32)
     both = both + lax.dot_general(exc, orb, turned, preferred_element_type=jnp.float32)
-    if lanes > n:
-        both = jnp.concatenate([both, jnp.zeros((n, lanes - n), jnp.float32)], axis=1)
-    part[...] = jnp.broadcast_to(both[:, None, :], part.shape)
-    each(lambda other, place: send(part.at[other], got, 2, other, place))
-    got[pl.ds(me, 1)] = part[pl.ds(me, 1)]
+    both = both * (0.5 / cells)
+    part[...] = jnp.concatenate([both[top : top + 8, :] for top in range(0, n, 8)], axis=1)
+    each(lambda other, place: send(part, got, 2, other, place))
+    got[pl.ds(me, 1)] = part[...][None]
     wait(got, 2)
-    line[...] = jnp.sum(got[...], axis=0)
-    each(lambda other, place: send(line, mat, 3, other, place))
-    mat[pl.ds(me, 1)] = line[...][None]
-    wait(mat, 3)
-    inverse = invert(mat, work, n, cells)[:, :n]
+    summed = jnp.sum(got[...], axis=0)
+    symmetric = jnp.concatenate([summed[:, left : left + n] for left in range(0, n * n // 8, n)], axis=0)
+    inverse = invert(symmetric, n)
     projected = dot(inverse, exc)
     for index in range(wide.shape[1]):
         wide[:, index, :] = projected[:, index * LANES : (index + 1) * LANES]
     proj[...] = wide[...].astype(jnp.bfloat16)
-    each(lambda other, place: send(proj.at[other], back, 4, other, place))
+    each(lambda other, place: send(proj.at[other], back, 3, other, place))
     back[pl.ds(me, 1)] = proj[pl.ds(me, 1)]
-    wait(back, 4)
+    wait(back, 3)
 
 
 def tail(orbital, exchange, cells):
     count, lines, _ = orbital.shape
     groups = lax.axis_size("grp")
-    lanes = -(-count // LANES) * LANES
+    packed = count * count // 8
     vmem = pl.BlockSpec(memory_space=pltpu.VMEM)
     slab = pltpu.VMEM(orbital.shape, jnp.bfloat16)
-    rows = pltpu.VMEM((count, 8, lanes), jnp.float32)
     return pl.pallas_call(
         functools.partial(tail_body, count, groups, cells),
         out_shape=jax.ShapeDtypeStruct(orbital.shape, jnp.bfloat16),
@@ -259,14 +244,11 @@
             slab,
             slab,
             pltpu.VMEM(orbital.shape, jnp.float32),
-            rows,
-            rows,
-            pltpu.VMEM((8, lanes), jnp.float32),
-            rows,
-            pltpu.VMEM((count, 2 * lanes), jnp.float32),
+            pltpu.VMEM((8, packed), jnp.float32),
+            pltpu.VMEM((count, 8, packed), jnp.float32),
             slab,
-            pltpu.SemaphoreType.DMA((5,)),
-            pltpu.SemaphoreType.DMA((5,)),
+            pltpu.SemaphoreType.DMA((4,)),
+            pltpu.SemaphoreType.DMA((4,)),
         ],
         compiler_params=pltpu.CompilerParams(
             collective_id=0, has_side_effects=True, vmem_limit_bytes=56 * 2**20
@@ -287,7 +269,7 @@
     parts = [orbitals] + [shifted(orbitals, "orb", step) for step in range(1, STEPS)]
     parts = [part.reshape(size * size, size) for part in parts]
     compact = exchange_of(parts, size)
-    if count <= LANES:
+    if count <= LANES // 2 and count % 32 == 0:
         lines = -(-cells // (count * LANES * 16)) * 16
         back = tail(to_pieces(orbitals, count, lines), to_pieces(compact, count, lines), cells)
         return back.reshape(count * lines, LANES)[: cells // LANES].reshape(1, cells)

time: 66.1 us -> 59.4 us (0.90)
  Pallas kernels: 48.2 us -> 41.6 us
    pallas_call x1, Pallas kernels: 36.9 us -> 30.2 us  [tail(): pl.pallas_call(functools.partial(tail_body, count, groups, cells), out_sh...]
where the time goes in v2:
time: 59.4 us; the launch traced here: 59.1 us
  Pallas kernels  41.6 us (70%)
  local copies, waits for them, and re-layouts  7.56 us (13%)
  waiting for transfers between devices  3.8 us (6%)
  other arithmetic  3.17 us (5%)
  starting transfers between devices  2.97 us (5%)
    pallas_call x1, Pallas kernels, tail(): pl.pallas_call(functools.partial(tail_body, count, groups, cells), out_sh...  30.2 us
    pallas_call x1, Pallas kernels, exchange_of(): pl.pallas_call(functools.partial(exchange_body, size), out_shape=jax.Shap...  11.4 us
    ppermute x2, waiting for transfers between devices, shifted(): return lax.ppermute(value, axis, pairs)  3.8 us
    unnamed x6, local copies, waits for them, and re-layouts  3.79 us
    ppermute x2, starting transfers between devices, shifted(): return lax.ppermute(value, axis, pairs)  2.97 us
    reshape x3, local copies, waits for them, and re-layouts, shards(): parts = [part.reshape(size * size, size) for part in parts]  1.84 us
    unnamed x1, other arithmetic  1.67 us
    ppermute x2, other arithmetic, shifted(): return lax.ppermute(value, axis, pairs)  1.5 us
  transfers between devices with their start and end apart: 2, of which 2 were waited for; matrix products, arithmetic and copies ran while one was open for 7% of the time, Pallas kernels for 0%

profile of v2, /device:TPU:0, one launch (start us, length us, event | category | flops | bytes accessed | tf_op | source)
XLA Modules:
  0.0 59.1 jit_solution(5097986150228324112)
XLA Ops:
  0.0 0.5 collective-permute-start
  0.5 2.5 %collective-permute-start.1 = (bf16[1,64000]{1,0:T(2,128)(2,1)}, bf16[1,64000]{1,0:T(2,128)(2,1)S(1)}, u32[]{:S(2)}, u32[]{:S(2)}) collective-permute-start(bf16[1,64000]{1,0:T(2,128)(2,1)} %param.5), channel_id=1, source_target_pairs={{0,8},{4,12},{8,16},{12,20},{16,24},{20,28},{24,0},{28,4},{1,9},{5... | collective-permute-start | bytes 384008 | tf_op jit(solution)/shard_map/ppermute | solution.py:21
  3.0 1.7 %reduce = bf16[64000]{0:T(1024)(128)(2,1)S(1)} reduce(bf16[1,64000]{1,0:T(2,128)(2,1)} %param.5, bf16[]{:T(256)} %constant.20), dimensions={0}, to_apply=%param.5.reduce_sub_computation | reduce | bytes 256002 | tf_op args[0]
  4.6 0.6 %reshape.29.refs_0_ = bf16[1600,40]{1,0:T(8,128)(2,1)S(1)} reshape(bf16[64000]{0:T(1024)(128)(2,1)S(1)} %reduce) | data formatting | bytes 256000 | tf_op jit(solution)/shard_map/reshape | solution.py:270
  5.3 0.7 %pad.7 = bf16[512,128]{1,0:T(8,128)(2,1)} pad(bf16[500,128]{1,0:T(8,128)(2,1)S(1)} %bitcast.10, bf16[]{:T(256)} %constant.10.clone.1), padding=0_12x0_0 | pad | bytes 259074 | tf_op jit(solution)/shard_map/jit(_pad)/pad | solution.py:261
  5.9 3.5 %collective-permute-done = bf16[1,64000]{1,0:T(2,128)(2,1)S(1)} collective-permute-done((bf16[1,64000]{1,0:T(2,128)(2,1)}, bf16[1,64000]{1,0:T(2,128)(2,1)S(1)}, u32[]{:S(2)}, u32[]{:S(2)}) %collective-permute-start) | collective-permute-done | bytes 128032 | tf_op jit(solution)/shard_map/ppermute | solution.py:21
  9.4 0.7 %reduce.2 = bf16[64000]{0:T(1024)(128)(2,1)S(1)} reduce(bf16[1,64000]{1,0:T(2,128)(2,1)S(1)} %collective-permute-done, bf16[]{:T(256)} %constant.20), dimensions={0}, to_apply=%ppermute.6.reduce_sub_computation | reduce | bytes 256002 | tf_op jit(solution)/shard_map/ppermute | solution.py:21
  10.2 0.6 %reshape.30.refs_1_ = bf16[1600,40]{1,0:T(8,128)(2,1)S(1)} reshape(bf16[64000]{0:T(1024)(128)(2,1)S(1)} %reduce.2) | data formatting | bytes 256000 | tf_op jit(solution)/shard_map/reshape | solution.py:270
  10.8 0.3 collective-permute-done.1
  11.1 0.7 %reduce.3 = bf16[64000]{0:T(1024)(128)(2,1)S(1)} reduce(bf16[1,64000]{1,0:T(2,128)(2,1)S(1)} %collective-permute-done.1, bf16[]{:T(256)} %constant.20), dimensions={0}, to_apply=%ppermute.7.reduce_sub_computation | reduce | bytes 256002 | tf_op jit(solution)/shard_map/ppermute | solution.py:21
  11.9 0.6 %reshape.31.refs_2_ = bf16[1600,40]{1,0:T(8,128)(2,1)S(1)} reshape(bf16[64000]{0:T(1024)(128)(2,1)S(1)} %reduce.3) | data formatting | bytes 256000 | tf_op jit(solution)/shard_map/reshape | solution.py:270
  12.5 0.0 copy-start
  12.5 1.1 %copy-done = f32[1600,128]{1,0:T(8,128)S(1)} copy-done((f32[1600,128]{1,0:T(8,128)S(1)}, f32[1600,128]{1,0:T(8,128)}, u32[]{:S(2)}) %copy-start) | copy-done | bytes 819224
  13.6 0.0 copy-start.1
  13.6 0.8 %copy-done.1 = bf16[128,256]{1,0:T(8,128)(2,1)S(1)} copy-done((bf16[128,256]{1,0:T(8,128)(2,1)S(1)}, bf16[128,256]{1,0:T(8,128)(2,1)}, u32[]{:S(2)}) %copy-start.1) | copy-done | bytes 65560
  14.5 11.4 %shard_map.55 = bf16[1600,40]{1,0:T(8,128)(2,1)S(1)} custom-call(bf16[1600,40]{1,0:T(8,128)(2,1)S(1)} %reshape.29.refs_0_, bf16[1600,40]{1,0:T(8,128)(2,1)S(1)} %reshape.30.refs_1_, bf16[1600,40]{1,0:T(8,128)(2,1)S(1)} %reshape.31.refs_2_, bf16[1600,1600]{1,0:T(8,128)(2,1)} %constant.11.clone.refs_3_, bf16[1600,1600]{1,0:T(8,128)(2,1)} %constant.12.clone.refs_4_, ...), custom_call_target="tpu_custom_call" | custom-call | tf_op jit(solution)/shard_map/pallas_call | solution.py:105
  25.8 0.6 %reshape.32 = bf16[500,128]{1,0:T(8,128)(2,1)S(1)} reshape(bf16[1600,40]{1,0:T(8,128)(2,1)S(1)} %shard_map.55) | data formatting | bytes 256000 | tf_op jit(solution)/shard_map/reshape | solution.py:260
  26.5 0.7 %pad.8 = bf16[512,128]{1,0:T(8,128)(2,1)} pad(bf16[500,128]{1,0:T(8,128)(2,1)S(1)} %reshape.32, bf16[]{:T(256)} %constant.10.clone.1), padding=0_12x0_0 | pad | bytes 259074 | tf_op jit(solution)/shard_map/jit(_pad)/pad | solution.py:261
  27.1 30.2 %shard_map.56 = bf16[32,16,128]{2,1,0:T(8,128)(2,1)} custom-call(bf16[32,16,128]{2,1,0:T(8,128)(2,1)} %bitcast.11, bf16[32,16,128]{2,1,0:T(8,128)(2,1)} %bitcast.12), custom_call_target="tpu_custom_call" | custom-call | tf_op jit(solution)/shard_map/pallas_call | solution.py:238
  57.3 0.9 %slice_bitcast_fusion = bf16[1,1,500,128]{3,2,1,0:T(8,128)(2,1)S(1)} fusion(bf16[512,128]{1,0:T(8,128)(2,1)} %bitcast.13), kind=kLoop, calls=%fused_computation.1 | loop fusion | bytes 256000
  58.2 0.9 %copy.8 = bf16[1,1,500,128]{3,1,2,0:T(2,128)(2,1)} copy(bf16[1,1,500,128]{3,2,1,0:T(8,128)(2,1)S(1)} %slice_bitcast_fusion) | data formatting | bytes 256000
Async XLA Ops:
  0.0 9.4 %collective-permute-start = (bf16[1,64000]{1,0:T(2,128)(2,1)}, bf16[1,64000]{1,0:T(2,128)(2,1)S(1)}, u32[]{:S(2)}, u32[]{:S(2)}) collective-permute-start(bf16[1,64000]{1,0:T(2,128)(2,1)} %param.5), channel_id=1, source_target_pairs={{0,4},{4,8},{8,12},{12,16},{16,20},{20,24},{24,28},{28,0},{1,5},{5... | collective-permute-start | bytes 384008 | tf_op jit(solution)/shard_map/ppermute | solution.py:21
  0.5 10.7 %collective-permute-start.1 = (bf16[1,64000]{1,0:T(2,128)(2,1)}, bf16[1,64000]{1,0:T(2,128)(2,1)S(1)}, u32[]{:S(2)}, u32[]{:S(2)}) collective-permute-start(bf16[1,64000]{1,0:T(2,128)(2,1)} %param.5), channel_id=1, source_target_pairs={{0,8},{4,12},{8,16},{12,20},{16,24},{20,28},{24,0},{28,4},{1,9},{5... | collective-permute-start | bytes 384008 | tf_op jit(solution)/shard_map/ppermute | solution.py:21
  12.5 1.1 %copy-start = (f32[1600,128]{1,0:T(8,128)S(1)}, f32[1600,128]{1,0:T(8,128)}, u32[]{:S(2)}) copy-start(f32[1600,128]{1,0:T(8,128)} %constant.14.clone.refs_6_) | copy-start | bytes 2457604
  13.6 0.8 %copy-start.1 = (bf16[128,256]{1,0:T(8,128)(2,1)S(1)}, bf16[128,256]{1,0:T(8,128)(2,1)}, u32[]{:S(2)}) copy-start(bf16[128,256]{1,0:T(8,128)(2,1)} %constant.13.clone.refs_5_) | copy-start | bytes 196612

commit v3 on v2

--- a/solution.py
+++ b/solution.py
@@ -115,6 +115,83 @@
     )(*parts, high, low, line, kernel)
 
 
+class Peers:
+    def __init__(self, count, groups, send_sem, recv_sem):
+        self.count, self.groups = count, groups
+        self.send_sem, self.recv_sem = send_sem, recv_sem
+        self.me = lax.axis_index("orb") * groups + lax.axis_index("grp")
+
+    def each(self, action):
+        def body(step, carry):
+            other = self.me + step
+            other = jnp.where(other >= self.count, other - self.count, other)
+            action(other, (lax.div(other, self.groups), lax.rem(other, self.groups)))
+            return carry
+
+        lax.fori_loop(1, self.count, body, 0, unroll=True)
+
+    def greet(self):
+        barrier = pltpu.get_barrier_semaphore()
+        self.each(
+            lambda other, place: pl.semaphore_signal(
+                barrier, inc=1, device_id=place, device_id_type=pl.DeviceIdType.MESH
+            )
+        )
+        pl.semaphore_wait(barrier, self.count - 1)
+
+    def send(self, source, target, slot, place):
+        pltpu.make_async_remote_copy(
+            src_ref=source,
+            dst_ref=target.at[self.me],
+            send_sem=self.send_sem.at[slot],
+            recv_sem=self.recv_sem.at[slot],
+            device_id=place,
+            device_id_type=pl.DeviceIdType.MESH,
+        ).start()
+
+    def wait(self, target, slot):
+        most = target.at[pl.ds(0, self.count - 1)]
+        pltpu.make_async_copy(most, most, self.recv_sem.at[slot]).wait()
+        pltpu.make_async_copy(most, most, self.send_sem.at[slot]).wait()
+
+
+def scatter_body(size, count, groups, *refs):
+    pieces, local, (out_ref, slab_out), rest = refs[0], refs[1 : STEPS + 5], refs[STEPS + 5 : STEPS + 7], refs[STEPS + 7 :]
+    store, pair, slab, send_sem, recv_sem = rest
+    peers = Peers(count, groups, send_sem, recv_sem)
+    peers.greet()
+    peers.each(lambda other, place: peers.send(pieces.at[other], slab, 0, place))
+    slab[pl.ds(peers.me, 1)] = pieces[pl.ds(peers.me, 1)]
+    exchange_body(size, *local, out_ref, store, pair)
+    peers.wait(slab, 0)
+    slab_out[...] = slab[...]
+
+
+def exchange_and_scatter(pieces, parts, size):
+    rows = size * size
+    high, low, line, kernel = tables(size)
+    vmem = pl.BlockSpec(memory_space=pltpu.VMEM)
+    return pl.pallas_call(
+        functools.partial(scatter_body, size, pieces.shape[0], lax.axis_size("grp")),
+        out_shape=(
+            jax.ShapeDtypeStruct((rows, size), jnp.bfloat16),
+            jax.ShapeDtypeStruct(pieces.shape, jnp.bfloat16),
+        ),
+        in_specs=[vmem] * (STEPS + 5),
+        out_specs=(vmem, vmem),
+        scratch_shapes=[
+            pltpu.VMEM((rows, LANES), jnp.float32),
+            pltpu.VMEM((rows, 2 * LANES), jnp.bfloat16),
+            pltpu.VMEM(pieces.shape, jnp.bfloat16),
+            pltpu.SemaphoreType.DMA((1,)),
+            pltpu.SemaphoreType.DMA((1,)),
+        ],
+        compiler_params=pltpu.CompilerParams(
+            collective_id=1, has_side_effects=True, vmem_limit_bytes=48 * 2**20
+        ),
+    )(pieces, *parts, high, low, line, kernel)
+
+
 def factorize(margin):
     symmetric = 0.5 * (margin + margin.T)
     magnitude = jnp.abs(symmetric)
@@ -158,65 +235,25 @@
     return jnp.concatenate(pieces, axis=1).astype(jnp.bfloat16)
 
 
-def tail_body(count, groups, cells, orbital, exchange, back, orb_slab, exc_slab, wide, part, got,
-              proj, send_sem, recv_sem):
+def tail_body(count, groups, cells, orbital, exchange, back, exc_slab, wide, part, got, proj,
+              send_sem, recv_sem):
     n = count
-    me = lax.axis_index("orb") * groups + lax.axis_index("grp")
-
-    def device(step):
-        other = me + step
-        other = jnp.where(other >= count, other - count, other)
-        return other, (lax.div(other, groups), lax.rem(other, groups))
-
-    def each(action):
-        def body(step, carry):
-            action(*device(step))
-            return carry
-
-        lax.fori_loop(1, count, body, 0)
-
-    def send(source, target, slot, other, place):
-        pltpu.make_async_remote_copy(
-            src_ref=source,
-            dst_ref=target.at[me],
-            send_sem=send_sem.at[slot],
-            recv_sem=recv_sem.at[slot],
-            device_id=place,
-            device_id_type=pl.DeviceIdType.MESH,
-        ).start()
-
-    def wait(target, slot):
-        most = target.at[pl.ds(0, count - 1)]
-        pltpu.make_async_copy(most, most, recv_sem.at[slot]).wait()
-        pltpu.make_async_copy(most, most, send_sem.at[slot]).wait()
-
-    barrier = pltpu.get_barrier_semaphore()
-    each(
-        lambda other, place: pl.semaphore_signal(
-            barrier, inc=1, device_id=place, device_id_type=pl.DeviceIdType.MESH
-        )
-    )
-    pl.semaphore_wait(barrier, count - 1)
-
-    def slabs(other, place):
-        send(exchange.at[other], exc_slab, 0, other, place)
-        send(orbital.at[other], orb_slab, 1, other, place)
-
-    each(slabs)
+    peers = Peers(count, groups, send_sem, recv_sem)
+    me = peers.me
+    peers.greet()
+    peers.each(lambda other, place: peers.send(exchange.at[other], exc_slab, 0, place))
     exc_slab[pl.ds(me, 1)] = exchange[pl.ds(me, 1)]
-    orb_slab[pl.ds(me, 1)] = orbital[pl.ds(me, 1)]
-    wait(exc_slab, 0)
-    wait(orb_slab, 1)
+    orb = flatten(wide, orbital)
+    peers.wait(exc_slab, 0)
     exc = flatten(wide, exc_slab)
-    orb = flatten(wide, orb_slab)
     turned = (((1,), (1,)), ((), ()))
     both = lax.dot_general(orb, exc, turned, preferred_element_type=jnp.float32)
     both = both + lax.dot_general(exc, orb, turned, preferred_element_type=jnp.float32)
     both = both * (0.5 / cells)
     part[...] = jnp.concatenate([both[top : top + 8, :] for top in range(0, n, 8)], axis=1)
-    each(lambda other, place: send(part, got, 2, other, place))
+    peers.each(lambda other, place: peers.send(part, got, 1, place))
     got[pl.ds(me, 1)] = part[...][None]
-    wait(got, 2)
+    peers.wait(got, 1)
     summed = jnp.sum(got[...], axis=0)
     symmetric = jnp.concatenate([summed[:, left : left + n] for left in range(0, n * n // 8, n)], axis=0)
     inverse = invert(symmetric, n)
@@ -224,9 +261,9 @@
     for index in range(wide.shape[1]):
         wide[:, index, :] = projected[:, index * LANES : (index + 1) * LANES]
     proj[...] = wide[...].astype(jnp.bfloat16)
-    each(lambda other, place: send(proj.at[other], back, 3, other, place))
+    peers.each(lambda other, place: peers.send(proj.at[other], back, 2, place))
     back[pl.ds(me, 1)] = proj[pl.ds(me, 1)]
-    wait(back, 3)
+    peers.wait(back, 2)
 
 
 def tail(orbital, exchange, cells):
@@ -242,13 +279,12 @@
         out_specs=vmem,
         scratch_shapes=[
             slab,
-            slab,
             pltpu.VMEM(orbital.shape, jnp.float32),
             pltpu.VMEM((8, packed), jnp.float32),
             pltpu.VMEM((count, 8, packed), jnp.float32),
             slab,
-            pltpu.SemaphoreType.DMA((4,)),
-            pltpu.SemaphoreType.DMA((4,)),
+            pltpu.SemaphoreType.DMA((3,)),
+            pltpu.SemaphoreType.DMA((3,)),
         ],
         compiler_params=pltpu.CompilerParams(
             collective_id=0, has_side_effects=True, vmem_limit_bytes=56 * 2**20
@@ -268,11 +304,12 @@
     count = lax.axis_size("orb") * lax.axis_size("grp")
     parts = [orbitals] + [shifted(orbitals, "orb", step) for step in range(1, STEPS)]
     parts = [part.reshape(size * size, size) for part in parts]
-    compact = exchange_of(parts, size)
     if count <= LANES // 2 and count % 32 == 0:
         lines = -(-cells // (count * LANES * 16)) * 16
-        back = tail(to_pieces(orbitals, count, lines), to_pieces(compact, count, lines), cells)
+        compact, slab = exchange_and_scatter(to_pieces(orbitals, count, lines), parts, size)
+        back = tail(slab, to_pieces(compact, count, lines), cells)
         return back.reshape(count * lines, LANES)[: cells // LANES].reshape(1, cells)
+    compact = exchange_of(parts, size)
     width = -(-cells // (count * LANES)) * LANES
     orbital_slab = to_slabs(orbitals, count, width)
     exchange_slab = to_slabs(compact.reshape(1, cells), count, width)

time: 59.4 us -> 60.9 us (1.025)
  Pallas kernels: 41.6 us -> 42.5 us
  waiting for transfers between devices: 3.8 us -> 4.45 us
    pallas_call x1, Pallas kernels: 11.4 us -> 18.2 us  [exchange_and_scatter(): pl.pallas_call(functools.partial(scatter_body, size, pieces.shape[0], lax...]
    pallas_call x1, Pallas kernels: 30.2 us -> 24.3 us  [tail(): pl.pallas_call(functools.partial(tail_body, count, groups, cells), out_sh...]
    pad x2, local copies, waits for them, and re-layouts: 1.32 us -> 0.66 us  [to_pieces(): padded = jnp.pad(tall, ((0, count * lines - tall.shape[0]), (0, 0)))]
    unnamed x6 -> x8, local copies, waits for them, and re-layouts: 3.79 us -> 4.44 us
    ppermute x2, waiting for transfers between devices: 3.8 us -> 4.45 us  [shifted(): return lax.ppermute(value, axis, pairs)]
  transfers between devices with their start and end apart: 2 -> 2, of which waited for: 2 -> 2; matrix products, arithmetic and copies ran while one was open for 7% -> 6% of each run, Pallas kernels for 0% -> 0%
where the time goes in v3:
time: 60.9 us; the launch traced here: 60.7 us
  Pallas kernels  42.5 us (70%)
  local copies, waits for them, and re-layouts  7.55 us (12%)
  waiting for transfers between devices  4.45 us (7%)
  other arithmetic  3.17 us (5%)
  starting transfers between devices  2.97 us (5%)
    pallas_call x1, Pallas kernels, tail(): pl.pallas_call(functools.partial(tail_body, count, groups, cells), out_sh...  24.3 us
    pallas_call x1, Pallas kernels, exchange_and_scatter(): pl.pallas_call(functools.partial(scatter_body, size, pieces.shape[0], lax...  18.2 us
    ppermute x2, waiting for transfers between devices, shifted(): return lax.ppermute(value, axis, pairs)  4.45 us
    unnamed x8, local copies, waits for them, and re-layouts  4.44 us
    ppermute x2, starting transfers between devices, shifted(): return lax.ppermute(value, axis, pairs)  2.97 us
    reshape x3, local copies, waits for them, and re-layouts, shards(): parts = [part.reshape(size * size, size) for part in parts]  1.84 us
    unnamed x1, other arithmetic  1.67 us
    ppermute x2, other arithmetic, shifted(): return lax.ppermute(value, axis, pairs)  1.5 us
  transfers between devices with their start and end apart: 2, of which 2 were waited for; matrix products, arithmetic and copies ran while one was open for 6% of the time, Pallas kernels for 0%

profile of v3, /device:TPU:0, one launch (start us, length us, event | category | flops | bytes accessed | tf_op | source)
XLA Modules:
  0.0 60.7 jit_solution(5043358079530673501)
XLA Ops:
  0.0 0.5 collective-permute-start
  0.5 2.5 %collective-permute-start.1 = (bf16[1,64000]{1,0:T(2,128)(2,1)}, bf16[1,64000]{1,0:T(2,128)(2,1)S(1)}, u32[]{:S(2)}, u32[]{:S(2)}) collective-permute-start(bf16[1,64000]{1,0:T(2,128)(2,1)} %param.5), channel_id=1, source_target_pairs={{0,8},{4,12},{8,16},{12,20},{16,24},{20,28},{24,0},{28,4},{1,9},{5... | collective-permute-start | bytes 384008 | tf_op jit(solution)/shard_map/ppermute | solution.py:21
  3.0 1.7 %reduce = bf16[64000]{0:T(1024)(128)(2,1)S(1)} reduce(bf16[1,64000]{1,0:T(2,128)(2,1)} %param.5, bf16[]{:T(256)} %constant.20), dimensions={0}, to_apply=%param.5.reduce_sub_computation | reduce | bytes 256002 | tf_op args[0]
  4.6 0.6 %reshape.29.refs_1_ = bf16[1600,40]{1,0:T(8,128)(2,1)S(1)} reshape(bf16[64000]{0:T(1024)(128)(2,1)S(1)} %reduce) | data formatting | bytes 256000 | tf_op jit(solution)/shard_map/reshape | solution.py:306
  5.3 4.1 %collective-permute-done = bf16[1,64000]{1,0:T(2,128)(2,1)S(1)} collective-permute-done((bf16[1,64000]{1,0:T(2,128)(2,1)}, bf16[1,64000]{1,0:T(2,128)(2,1)S(1)}, u32[]{:S(2)}, u32[]{:S(2)}) %collective-permute-start) | collective-permute-done | bytes 128032 | tf_op jit(solution)/shard_map/ppermute | solution.py:21
  9.4 0.7 %reduce.2 = bf16[64000]{0:T(1024)(128)(2,1)S(1)} reduce(bf16[1,64000]{1,0:T(2,128)(2,1)S(1)} %collective-permute-done, bf16[]{:T(256)} %constant.20), dimensions={0}, to_apply=%ppermute.6.reduce_sub_computation | reduce | bytes 256002 | tf_op jit(solution)/shard_map/ppermute | solution.py:21
  10.2 0.6 %reshape.30.refs_2_ = bf16[1600,40]{1,0:T(8,128)(2,1)S(1)} reshape(bf16[64000]{0:T(1024)(128)(2,1)S(1)} %reduce.2) | data formatting | bytes 256000 | tf_op jit(solution)/shard_map/reshape | solution.py:306
  10.8 0.3 collective-permute-done.1
  11.1 0.7 %reduce.3 = bf16[64000]{0:T(1024)(128)(2,1)S(1)} reduce(bf16[1,64000]{1,0:T(2,128)(2,1)S(1)} %collective-permute-done.1, bf16[]{:T(256)} %constant.20), dimensions={0}, to_apply=%ppermute.7.reduce_sub_computation | reduce | bytes 256002 | tf_op jit(solution)/shard_map/ppermute | solution.py:21
  11.9 0.6 %reshape.31.refs_3_ = bf16[1600,40]{1,0:T(8,128)(2,1)S(1)} reshape(bf16[64000]{0:T(1024)(128)(2,1)S(1)} %reduce.3) | data formatting | bytes 256000 | tf_op jit(solution)/shard_map/reshape | solution.py:306
  12.5 0.0 copy-start
  12.5 1.1 %copy-done = f32[1600,128]{1,0:T(8,128)S(1)} copy-done((f32[1600,128]{1,0:T(8,128)S(1)}, f32[1600,128]{1,0:T(8,128)}, u32[]{:S(2)}) %copy-start) | copy-done | bytes 819224
  13.6 0.0 copy-start.2
  13.6 0.8 %copy-done.2 = bf16[128,256]{1,0:T(8,128)(2,1)S(1)} copy-done((bf16[128,256]{1,0:T(8,128)(2,1)S(1)}, bf16[128,256]{1,0:T(8,128)(2,1)}, u32[]{:S(2)}) %copy-start.2) | copy-done | bytes 65560
  14.5 18.2 %shard_map.55 = (bf16[1600,40]{1,0:T(8,128)(2,1)S(1)}, bf16[32,16,128]{2,1,0:T(8,128)(2,1)S(1)}) custom-call(bf16[32,16,128]{2,1,0:T(8,128)(2,1)S(1)} %bitcast.10, bf16[1600,40]{1,0:T(8,128)(2,1)S(1)} %reshape.29.refs_1_, bf16[1600,40]{1,0:T(8,128)(2,1)S(1)} %reshape.30.refs_2_, bf16[1600,40]{1,0:T(8,128)(2,1)S(1)} %reshape.31.refs_3_, ...), custom_call_target="tpu_custom_call" | custom-call | tf_op jit(solution)/shard_map/pallas_call | solution.py:174
  32.7 0.0 copy-start.1
  32.7 0.6 %copy-done.1 = bf16[32,16,128]{2,1,0:T(8,128)(2,1)} copy-done((bf16[32,16,128]{2,1,0:T(8,128)(2,1)}, bf16[32,16,128]{2,1,0:T(8,128)(2,1)S(1)}, u32[]{:S(2)}) %copy-start.1) | copy-done | bytes 131096
  33.3 0.6 %reshape.32 = bf16[500,128]{1,0:T(8,128)(2,1)S(1)} reshape(bf16[1600,40]{1,0:T(8,128)(2,1)S(1)} %get-tuple-element.8) | data formatting | bytes 256000 | tf_op jit(solution)/shard_map/reshape | solution.py:296
  33.9 0.7 %pad.8 = bf16[512,128]{1,0:T(8,128)(2,1)} pad(bf16[500,128]{1,0:T(8,128)(2,1)S(1)} %reshape.32, bf16[]{:T(256)} %constant.10.clone.1), padding=0_12x0_0 | pad | bytes 259074 | tf_op jit(solution)/shard_map/jit(_pad)/pad | solution.py:297
  34.6 24.3 %shard_map.56 = bf16[32,16,128]{2,1,0:T(8,128)(2,1)} custom-call(bf16[32,16,128]{2,1,0:T(8,128)(2,1)} %copy-done.1, bf16[32,16,128]{2,1,0:T(8,128)(2,1)} %bitcast.12), custom_call_target="tpu_custom_call" | custom-call | tf_op jit(solution)/shard_map/pallas_call | solution.py:275
  58.9 0.9 %slice_bitcast_fusion = bf16[1,1,500,128]{3,2,1,0:T(8,128)(2,1)S(1)} fusion(bf16[512,128]{1,0:T(8,128)(2,1)} %bitcast.13), kind=kLoop, calls=%fused_computation.1 | loop fusion | bytes 256000
  59.8 0.9 %copy.8 = bf16[1,1,500,128]{3,1,2,0:T(2,128)(2,1)} copy(bf16[1,1,500,128]{3,2,1,0:T(8,128)(2,1)S(1)} %slice_bitcast_fusion) | data formatting | bytes 256000
  (1 shorter events, 0.0 us)
Async XLA Ops:
  0.0 9.4 %collective-permute-start = (bf16[1,64000]{1,0:T(2,128)(2,1)}, bf16[1,64000]{1,0:T(2,128)(2,1)S(1)}, u32[]{:S(2)}, u32[]{:S(2)}) collective-permute-start(bf16[1,64000]{1,0:T(2,128)(2,1)} %param.5), channel_id=1, source_target_pairs={{0,4},{4,8},{8,12},{12,16},{16,20},{20,24},{24,28},{28,0},{1,5},{5... | collective-permute-start | bytes 384008 | tf_op jit(solution)/shard_map/ppermute | solution.py:21
  0.5 10.7 %collective-permute-start.1 = (bf16[1,64000]{1,0:T(2,128)(2,1)}, bf16[1,64000]{1,0:T(2,128)(2,1)S(1)}, u32[]{:S(2)}, u32[]{:S(2)}) collective-permute-start(bf16[1,64000]{1,0:T(2,128)(2,1)} %param.5), channel_id=1, source_target_pairs={{0,8},{4,12},{8,16},{12,20},{16,24},{20,28},{24,0},{28,4},{1,9},{5... | collective-permute-start | bytes 384008 | tf_op jit(solution)/shard_map/ppermute | solution.py:21
  12.5 1.1 %copy-start = (f32[1600,128]{1,0:T(8,128)S(1)}, f32[1600,128]{1,0:T(8,128)}, u32[]{:S(2)}) copy-start(f32[1600,128]{1,0:T(8,128)} %constant.14.clone.refs_7_) | copy-start | bytes 2457604
  13.6 0.8 %copy-start.2 = (bf16[128,256]{1,0:T(8,128)(2,1)S(1)}, bf16[128,256]{1,0:T(8,128)(2,1)}, u32[]{:S(2)}) copy-start(bf16[128,256]{1,0:T(8,128)(2,1)} %constant.13.clone.refs_6_) | copy-start | bytes 196612
  32.7 0.7 %copy-start.1 = (bf16[32,16,128]{2,1,0:T(8,128)(2,1)}, bf16[32,16,128]{2,1,0:T(8,128)(2,1)S(1)}, u32[]{:S(2)}) copy-start(bf16[32,16,128]{2,1,0:T(8,128)(2,1)S(1)} %get-tuple-element.7.orbital) | copy-start | bytes 393220

commit v4 on v2

--- a/solution.py
+++ b/solution.py
@@ -79,7 +79,13 @@
 
 def exchange_body(size, *refs):
     parts = refs[:STEPS]
-    high_ref, low_ref, line_ref, kernel_ref, out_ref, store, pair = refs[STEPS:]
+    high_far, low_far, line_ref, kernel_ref, out_ref, store, pair, high_ref, low_ref, sems = refs[STEPS:]
+    copies = [
+        pltpu.make_async_copy(high_far, high_ref, sems.at[0]),
+        pltpu.make_async_copy(low_far, low_ref, sems.at[1]),
+    ]
+    for copy in copies:
+        copy.start()
     rows = size * size
     block = rows // 5 if rows % 40 == 0 else rows
     values = [part[...].astype(jnp.float32) for part in parts]
@@ -88,6 +94,8 @@
     target = jnp.concatenate([values[0]] * STEPS + [spare], axis=1)
     line = line_ref[...]
     put_pair(pair, line_transform(target * source, line))
+    for copy in copies:
+        copy.wait()
     plane_transform(store, high_ref, low_ref, pair, rows, block, kernel_ref)
     put_pair(pair, store[...])
     plane_transform(store, high_ref, low_ref, pair, rows, block)
@@ -105,13 +113,16 @@
     return pl.pallas_call(
         functools.partial(exchange_body, size),
         out_shape=jax.ShapeDtypeStruct((rows, size), jnp.bfloat16),
-        in_specs=[vmem] * (STEPS + 4),
+        in_specs=[vmem] * STEPS + [pl.BlockSpec(memory_space=pl.ANY)] * 2 + [vmem] * 2,
         out_specs=vmem,
         scratch_shapes=[
             pltpu.VMEM((rows, LANES), jnp.float32),
             pltpu.VMEM((rows, 2 * LANES), jnp.bfloat16),
+            pltpu.VMEM((rows, rows), jnp.bfloat16),
+            pltpu.VMEM((rows, rows), jnp.bfloat16),
+            pltpu.SemaphoreType.DMA((2,)),
         ],
-        compiler_params=pltpu.CompilerParams(vmem_limit_bytes=48 * 2**20),
+        compiler_params=pltpu.CompilerParams(vmem_limit_bytes=58 * 2**20),
     )(*parts, high, low, line, kernel)
 
 
@@ -199,16 +210,16 @@
     pl.semaphore_wait(barrier, count - 1)
 
     def slabs(other, place):
-        send(exchange.at[other], exc_slab, 0, other, place)
         send(orbital.at[other], orb_slab, 1, other, place)
 
     each(slabs)
+    each(lambda other, place: send(exchange.at[other], exc_slab, 0, other, place))
     exc_slab[pl.ds(me, 1)] = exchange[pl.ds(me, 1)]
     orb_slab[pl.ds(me, 1)] = orbital[pl.ds(me, 1)]
+    wait(orb_slab, 1)
+    orb = flatten(wide, orb_slab)
     wait(exc_slab, 0)
-    wait(orb_slab, 1)
     exc = flatten(wide, exc_slab)
-    orb = flatten(wide, orb_slab)
     turned = (((1,), (1,)), ((), ()))
     both = lax.dot_general(orb, exc, turned, preferred_element_type=jnp.float32)
     both = both + lax.dot_general(exc, orb, turned, preferred_element_type=jnp.float32)
@@ -266,12 +277,15 @@
     cells = orbitals.shape[1]
     size = round(cells ** (1.0 / 3.0))
     count = lax.axis_size("orb") * lax.axis_size("grp")
-    parts = [orbitals] + [shifted(orbitals, "orb", step) for step in range(1, STEPS)]
+    tall = lax.optimization_barrier(orbitals.reshape(-1, LANES))
+    parts = [tall] + [
+        lax.optimization_barrier(shifted(tall, "orb", step)) for step in range(1, STEPS)
+    ]
     parts = [part.reshape(size * size, size) for part in parts]
     compact = exchange_of(parts, size)
     if count <= LANES // 2 and count % 32 == 0:
         lines = -(-cells // (count * LANES * 16)) * 16
-        back = tail(to_pieces(orbitals, count, lines), to_pieces(compact, count, lines), cells)
+        back = tail(to_pieces(tall, count, lines), to_pieces(compact, count, lines), cells)
         return back.reshape(count * lines, LANES)[: cells // LANES].reshape(1, cells)
     width = -(-cells // (count * LANES)) * LANES
     orbital_slab = to_slabs(orbitals, count, width)

time: 59.4 us -> 57.9 us (0.975)
  waiting for transfers between devices: 3.8 us -> 1.75 us
  other arithmetic: 3.17 us -> 1.66 us
  local copies, waits for them, and re-layouts: 7.56 us -> 8.8 us
  Pallas kernels: 41.6 us -> 42.4 us
    reshape x3, local copies, waits for them, and re-layouts: 1.84 us -> 4.07 us  [shards(): parts = [part.reshape(size * size, size) for part in parts]]
    ppermute x2, waiting for transfers between devices: 3.8 us -> 1.75 us  [shifted(): return lax.ppermute(value, axis, pairs)]
    unnamed x6 -> x2, local copies, waits for them, and re-layouts: 3.79 us -> 1.81 us
    pallas_call x1, Pallas kernels: 11.4 us -> 13 us  [exchange_of(): pl.pallas_call(functools.partial(exchange_body, size), out_shape=jax.Shap...]
    ppermute x2 -> x0, other arithmetic: 1.5 us -> none  [shifted(): return lax.ppermute(value, axis, pairs)]
    reshape x1, local copies, waits for them, and re-layouts: 0.61 us -> 1.61 us  [to_pieces(): tall = flat.reshape(-1, LANES)]
    pallas_call x1, Pallas kernels: 30.2 us -> 29.4 us  [tail(): pl.pallas_call(functools.partial(tail_body, count, groups, cells), out_sh...]
  transfers between devices with their start and end apart: 2 -> 2, of which waited for: 2 -> 2; matrix products, arithmetic and copies ran while one was open for 7% -> 6% of each run, Pallas kernels for 0% -> 0%
where the time goes in v4:
time: 57.9 us; the launch traced here: 57.7 us
  Pallas kernels  42.4 us (73%)
  local copies, waits for them, and re-layouts  8.8 us (15%)
  starting transfers between devices  3.06 us (5%)
  waiting for transfers between devices  1.75 us (3%)
  other arithmetic  1.66 us (3%)
    pallas_call x1, Pallas kernels, tail(): pl.pallas_call(functools.partial(tail_body, count, groups, cells), out_sh...  29.4 us
    pallas_call x1, Pallas kernels, exchange_of(): pl.pallas_call(functools.partial(exchange_body, size), out_shape=jax.Shap...  13 us
    reshape x3, local copies, waits for them, and re-layouts, shards(): parts = [part.reshape(size * size, size) for part in parts]  4.07 us
    ppermute x2, starting transfers between devices, shifted(): return lax.ppermute(value, axis, pairs)  3.06 us
    unnamed x2, local copies, waits for them, and re-layouts  1.81 us
    ppermute x2, waiting for transfers between devices, shifted(): return lax.ppermute(value, axis, pairs)  1.75 us
    unnamed x1, other arithmetic  1.66 us
    reshape x1, local copies, waits for them, and re-layouts, to_pieces(): tall = flat.reshape(-1, LANES)  1.61 us
  transfers between devices with their start and end apart: 2, of which 2 were waited for; matrix products, arithmetic and copies ran while one was open for 6% of the time, Pallas kernels for 0%

profile of v4, /device:TPU:0, one launch (start us, length us, event | category | flops | bytes accessed | tf_op | source)
XLA Modules:
  0.0 57.7 jit_solution(17040527281377977428)
XLA Ops:
  0.0 1.7 %reduce = bf16[64000]{0:T(1024)(128)(2,1)S(1)} reduce(bf16[1,64000]{1,0:T(2,128)(2,1)} %param.5, bf16[]{:T(256)} %constant.20), dimensions={0}, to_apply=%param.5.reduce_sub_computation | reduce | bytes 256002 | tf_op args[0]
  1.7 0.5 collective-permute-start
  2.2 2.6 %collective-permute-start.1 = (bf16[500,128]{1,0:T(8,128)(2,1)S(1)}, bf16[500,128]{1,0:T(8,128)(2,1)S(1)}, u32[]{:S(2)}, u32[]{:S(2)}) collective-permute-start(bf16[500,128]{1,0:T(8,128)(2,1)S(1)} %bitcast.11), channel_id=1, source_target_pairs={{0,8},{4,12},{8,16},{12,20},{16,24},{20,28},{24,0},{28,4},{1,9},{5... | collective-permute-start | bytes 384008 | tf_op jit(solution)/shard_map/ppermute | solution.py:21
  4.7 1.4 %reshape.29.refs_0_ = bf16[1600,40]{1,0:T(8,128)(2,1)} reshape(bf16[500,128]{1,0:T(8,128)(2,1)S(1)} %bitcast.12) | data formatting | bytes 256000 | tf_op jit(solution)/shard_map/reshape | solution.py:284
  6.1 0.7 %pad.7 = bf16[512,128]{1,0:T(8,128)(2,1)} pad(bf16[500,128]{1,0:T(8,128)(2,1)S(1)} %bitcast.13, bf16[]{:T(256)} %constant.10.clone.1), padding=0_12x0_0 | pad | bytes 259074 | tf_op jit(solution)/shard_map/jit(_pad)/pad | solution.py:272
  6.7 1.4 %collective-permute-done = bf16[500,128]{1,0:T(8,128)(2,1)S(1)} collective-permute-done((bf16[500,128]{1,0:T(8,128)(2,1)S(1)}, bf16[500,128]{1,0:T(8,128)(2,1)S(1)}, u32[]{:S(2)}, u32[]{:S(2)}) %collective-permute-start) | collective-permute-done | bytes 128032 | tf_op jit(solution)/shard_map/ppermute | solution.py:21
  8.1 1.4 %reshape.30.refs_1_ = bf16[1600,40]{1,0:T(8,128)(2,1)} reshape(bf16[500,128]{1,0:T(8,128)(2,1)S(1)} %collective-permute-done) | data formatting | bytes 256000 | tf_op jit(solution)/shard_map/reshape | solution.py:284
  9.5 0.3 collective-permute-done.1
  9.8 1.4 %reshape.31.refs_2_ = bf16[1600,40]{1,0:T(8,128)(2,1)} reshape(bf16[500,128]{1,0:T(8,128)(2,1)S(1)} %collective-permute-done.1) | data formatting | bytes 256000 | tf_op jit(solution)/shard_map/reshape | solution.py:284
  11.2 13.0 %shard_map.55 = bf16[1600,40]{1,0:T(8,128)(2,1)} custom-call(bf16[1600,40]{1,0:T(8,128)(2,1)} %reshape.29.refs_0_, bf16[1600,40]{1,0:T(8,128)(2,1)} %reshape.30.refs_1_, bf16[1600,40]{1,0:T(8,128)(2,1)} %reshape.31.refs_2_, bf16[1600,1600]{1,0:T(8,128)(2,1)} %constant.11.clone.refs_3_, bf16[1600,1600]{1,0:T(8,128)(2,1)} %constant.12.clone.refs_4_, ...), custom_call_target="tpu_custom_call" | custom-call | tf_op jit(solution)/shard_map/pallas_call | solution.py:113
  24.2 1.6 %reshape.32 = bf16[500,128]{1,0:T(8,128)(2,1)S(1)} reshape(bf16[1600,40]{1,0:T(8,128)(2,1)} %shard_map.55) | data formatting | bytes 256000 | tf_op jit(solution)/shard_map/reshape | solution.py:271
  25.8 0.7 %pad.8 = bf16[512,128]{1,0:T(8,128)(2,1)} pad(bf16[500,128]{1,0:T(8,128)(2,1)S(1)} %reshape.32, bf16[]{:T(256)} %constant.10.clone.1), padding=0_12x0_0 | pad | bytes 259074 | tf_op jit(solution)/shard_map/jit(_pad)/pad | solution.py:272
  26.4 29.4 %shard_map.56 = bf16[32,16,128]{2,1,0:T(8,128)(2,1)} custom-call(bf16[32,16,128]{2,1,0:T(8,128)(2,1)} %bitcast.14, bf16[32,16,128]{2,1,0:T(8,128)(2,1)} %bitcast.15), custom_call_target="tpu_custom_call" | custom-call | tf_op jit(solution)/shard_map/pallas_call | solution.py:249
  55.9 0.9 %slice_bitcast_fusion = bf16[1,1,500,128]{3,2,1,0:T(8,128)(2,1)S(1)} fusion(bf16[512,128]{1,0:T(8,128)(2,1)} %bitcast.16), kind=kLoop, calls=%fused_computation.1 | loop fusion | bytes 256000
  56.8 0.9 %copy.8 = bf16[1,1,500,128]{3,1,2,0:T(2,128)(2,1)} copy(bf16[1,1,500,128]{3,2,1,0:T(8,128)(2,1)S(1)} %slice_bitcast_fusion) | data formatting | bytes 256000
Async XLA Ops:
  1.7 6.5 %collective-permute-start = (bf16[500,128]{1,0:T(8,128)(2,1)S(1)}, bf16[500,128]{1,0:T(8,128)(2,1)S(1)}, u32[]{:S(2)}, u32[]{:S(2)}) collective-permute-start(bf16[500,128]{1,0:T(8,128)(2,1)S(1)} %bitcast.10), channel_id=1, source_target_pairs={{0,4},{4,8},{8,12},{12,16},{16,20},{20,24},{24,28},{28,0},{1,5},{5... | collective-permute-start | bytes 384008 | tf_op jit(solution)/shard_map/ppermute | solution.py:21
  2.2 7.7 %collective-permute-start.1 = (bf16[500,128]{1,0:T(8,128)(2,1)S(1)}, bf16[500,128]{1,0:T(8,128)(2,1)S(1)}, u32[]{:S(2)}, u32[]{:S(2)}) collective-permute-start(bf16[500,128]{1,0:T(8,128)(2,1)S(1)} %bitcast.11), channel_id=1, source_target_pairs={{0,8},{4,12},{8,16},{12,20},{16,24},{20,28},{24,0},{28,4},{1,9},{5... | collective-permute-start | bytes 384008 | tf_op jit(solution)/shard_map/ppermute | solution.py:21

commit v5 on v4

--- a/solution.py
+++ b/solution.py
@@ -184,7 +184,7 @@
             action(*device(step))
             return carry
 
-        lax.fori_loop(1, count, body, 0)
+        lax.fori_loop(1, count, body, 0, unroll=True)
 
     def send(source, target, slot, other, place):
         pltpu.make_async_remote_copy(

time: 57.9 us -> 57.9 us (level)
  no operation moved by 1% of the time
where the time goes in v5:
time: 57.9 us; the launch traced here: 57.6 us
  Pallas kernels  42.3 us (73%)
  local copies, waits for them, and re-layouts  8.8 us (15%)
  starting transfers between devices  3.06 us (5%)
  waiting for transfers between devices  1.75 us (3%)
  other arithmetic  1.66 us (3%)
    pallas_call x1, Pallas kernels, tail(): pl.pallas_call(functools.partial(tail_body, count, groups, cells), out_sh...  29.4 us
    pallas_call x1, Pallas kernels, exchange_of(): pl.pallas_call(functools.partial(exchange_body, size), out_shape=jax.Shap...  13 us
    reshape x3, local copies, waits for them, and re-layouts, shards(): parts = [part.reshape(size * size, size) for part in parts]  4.07 us
    ppermute x2, starting transfers between devices, shifted(): return lax.ppermute(value, axis, pairs)  3.06 us
    unnamed x2, local copies, waits for them, and re-layouts  1.81 us
    ppermute x2, waiting for transfers between devices, shifted(): return lax.ppermute(value, axis, pairs)  1.75 us
    unnamed x1, other arithmetic  1.66 us
    reshape x1, local copies, waits for them, and re-layouts, to_pieces(): tall = flat.reshape(-1, LANES)  1.61 us
  transfers between devices with their start and end apart: 2, of which 2 were waited for; matrix products, arithmetic and copies ran while one was open for 6% of the time, Pallas kernels for 0%

profile of v5, /device:TPU:0, one launch (start us, length us, event | category | flops | bytes accessed | tf_op | source)
XLA Modules:
  0.0 57.6 jit_solution(7374217214119493224)
XLA Ops:
  0.0 1.7 %reduce = bf16[64000]{0:T(1024)(128)(2,1)S(1)} reduce(bf16[1,64000]{1,0:T(2,128)(2,1)} %param.5, bf16[]{:T(256)} %constant.20), dimensions={0}, to_apply=%param.5.reduce_sub_computation | reduce | bytes 256002 | tf_op args[0]
  1.7 0.5 collective-permute-start
  2.2 2.6 %collective-permute-start.1 = (bf16[500,128]{1,0:T(8,128)(2,1)S(1)}, bf16[500,128]{1,0:T(8,128)(2,1)S(1)}, u32[]{:S(2)}, u32[]{:S(2)}) collective-permute-start(bf16[500,128]{1,0:T(8,128)(2,1)S(1)} %bitcast.11), channel_id=1, source_target_pairs={{0,8},{4,12},{8,16},{12,20},{16,24},{20,28},{24,0},{28,4},{1,9},{5... | collective-permute-start | bytes 384008 | tf_op jit(solution)/shard_map/ppermute | solution.py:21
  4.7 1.4 %reshape.29.refs_0_ = bf16[1600,40]{1,0:T(8,128)(2,1)} reshape(bf16[500,128]{1,0:T(8,128)(2,1)S(1)} %bitcast.12) | data formatting | bytes 256000 | tf_op jit(solution)/shard_map/reshape | solution.py:284
  6.1 0.7 %pad.7 = bf16[512,128]{1,0:T(8,128)(2,1)} pad(bf16[500,128]{1,0:T(8,128)(2,1)S(1)} %bitcast.13, bf16[]{:T(256)} %constant.10.clone.1), padding=0_12x0_0 | pad | bytes 259074 | tf_op jit(solution)/shard_map/jit(_pad)/pad | solution.py:272
  6.7 1.4 %collective-permute-done = bf16[500,128]{1,0:T(8,128)(2,1)S(1)} collective-permute-done((bf16[500,128]{1,0:T(8,128)(2,1)S(1)}, bf16[500,128]{1,0:T(8,128)(2,1)S(1)}, u32[]{:S(2)}, u32[]{:S(2)}) %collective-permute-start) | collective-permute-done | bytes 128032 | tf_op jit(solution)/shard_map/ppermute | solution.py:21
  8.1 1.4 %reshape.30.refs_1_ = bf16[1600,40]{1,0:T(8,128)(2,1)} reshape(bf16[500,128]{1,0:T(8,128)(2,1)S(1)} %collective-permute-done) | data formatting | bytes 256000 | tf_op jit(solution)/shard_map/reshape | solution.py:284
  9.5 0.3 collective-permute-done.1
  9.8 1.4 %reshape.31.refs_2_ = bf16[1600,40]{1,0:T(8,128)(2,1)} reshape(bf16[500,128]{1,0:T(8,128)(2,1)S(1)} %collective-permute-done.1) | data formatting | bytes 256000 | tf_op jit(solution)/shard_map/reshape | solution.py:284
  11.2 13.0 %shard_map.55 = bf16[1600,40]{1,0:T(8,128)(2,1)} custom-call(bf16[1600,40]{1,0:T(8,128)(2,1)} %reshape.29.refs_0_, bf16[1600,40]{1,0:T(8,128)(2,1)} %reshape.30.refs_1_, bf16[1600,40]{1,0:T(8,128)(2,1)} %reshape.31.refs_2_, bf16[1600,1600]{1,0:T(8,128)(2,1)} %constant.11.clone.refs_3_, bf16[1600,1600]{1,0:T(8,128)(2,1)} %constant.12.clone.refs_4_, ...), custom_call_target="tpu_custom_call" | custom-call | tf_op jit(solution)/shard_map/pallas_call | solution.py:113
  24.2 1.6 %reshape.32 = bf16[500,128]{1,0:T(8,128)(2,1)S(1)} reshape(bf16[1600,40]{1,0:T(8,128)(2,1)} %shard_map.55) | data formatting | bytes 256000 | tf_op jit(solution)/shard_map/reshape | solution.py:271
  25.8 0.7 %pad.8 = bf16[512,128]{1,0:T(8,128)(2,1)} pad(bf16[500,128]{1,0:T(8,128)(2,1)S(1)} %reshape.32, bf16[]{:T(256)} %constant.10.clone.1), padding=0_12x0_0 | pad | bytes 259074 | tf_op jit(solution)/shard_map/jit(_pad)/pad | solution.py:272
  26.4 29.4 %shard_map.56 = bf16[32,16,128]{2,1,0:T(8,128)(2,1)} custom-call(bf16[32,16,128]{2,1,0:T(8,128)(2,1)} %bitcast.14, bf16[32,16,128]{2,1,0:T(8,128)(2,1)} %bitcast.15), custom_call_target="tpu_custom_call" | custom-call | tf_op jit(solution)/shard_map/pallas_call | solution.py:249
  55.8 0.9 %slice_bitcast_fusion = bf16[1,1,500,128]{3,2,1,0:T(8,128)(2,1)S(1)} fusion(bf16[512,128]{1,0:T(8,128)(2,1)} %bitcast.16), kind=kLoop, calls=%fused_computation.1 | loop fusion | bytes 256000
  56.8 0.9 %copy.8 = bf16[1,1,500,128]{3,1,2,0:T(2,128)(2,1)} copy(bf16[1,1,500,128]{3,2,1,0:T(8,128)(2,1)S(1)} %slice_bitcast_fusion) | data formatting | bytes 256000
Async XLA Ops:
  1.7 6.5 %collective-permute-start = (bf16[500,128]{1,0:T(8,128)(2,1)S(1)}, bf16[500,128]{1,0:T(8,128)(2,1)S(1)}, u32[]{:S(2)}, u32[]{:S(2)}) collective-permute-start(bf16[500,128]{1,0:T(8,128)(2,1)S(1)} %bitcast.10), channel_id=1, source_target_pairs={{0,4},{4,8},{8,12},{12,16},{16,20},{20,24},{24,28},{28,0},{1,5},{5... | collective-permute-start | bytes 384008 | tf_op jit(solution)/shard_map/ppermute | solution.py:21
  2.2 7.7 %collective-permute-start.1 = (bf16[500,128]{1,0:T(8,128)(2,1)S(1)}, bf16[500,128]{1,0:T(8,128)(2,1)S(1)}, u32[]{:S(2)}, u32[]{:S(2)}) collective-permute-start(bf16[500,128]{1,0:T(8,128)(2,1)S(1)} %bitcast.11), channel_id=1, source_target_pairs={{0,8},{4,12},{8,16},{12,20},{16,24},{20,28},{24,0},{28,4},{1,9},{5... | collective-permute-start | bytes 384008 | tf_op jit(solution)/shard_map/ppermute | solution.py:21
